TPU v7x, 512 devices: a whole 4x8x8 slice. The times are simulated.
512 devices in a mesh: rep: 64 (over x, y, core), tp: 8 (over z).
Axes of the slice: x: 4, y: 8, z: 8, core: 2. Of those that a mesh axis runs over, the one named last changes fastest.
Arguments:
- queries: bfloat16 [16384, 4096], P('rep', 'tp'), may hold values from -8 to 8
- suffix_key_rows: bfloat16 [16384, 1024], P('rep', 'tp'), may hold values from -8 to 8
- suffix_value_rows: bfloat16 [16384, 1024], P('rep', 'tp'), may hold values from -6 to 6
- mamba_input: bfloat16 [16384, 8192], P('rep', 'tp'), may hold values from -6 to 6
- mamba_gate: bfloat16 [16384, 8192], P('rep', 'tp'), may hold values from -18 to 18
- input_projection: bfloat16 [16384, 256], P('rep'), may hold values from -6 to 6
- output_projection: bfloat16 [16384, 256], P('rep'), may hold values from -6 to 6
- step_lengths: float32 [16384, 128], P('rep', 'tp'), may hold values from 0.0002 to 1
- decay_log: float32 [128], P('tp'), may hold values from -0.7 to 2.8
- skip_gain: float32 [128], P('tp'), may hold values from 0.5 to 1.5
- gated_norm_gain: float32 [8192], P('tp'), may hold values from 0.5 to 1.5
- cache_store: bfloat16 [1024, 8, 2, 128, 128], P('rep', 'tp'), may hold values from -6 to 6
- request_units: int32 [128, 56], replicated, may hold values from 0 to 1023, as said below
- prefix_block_count: int32 [128], replicated, may hold values from 8 to 48
Outputs:
- attn_out: bfloat16 [16384, 4096], P('rep', 'tp')
- mamba_out: bfloat16 [16384, 8192], P('rep', 'tp')
- final_state: bfloat16 [128, 128, 64, 256], P('rep', 'tp')
Inputs may be any that keep to these rules, and one draw needn't show every extreme that they name: `request_units`: entries 0 to 47 of row q name request q's prefix blocks in order, of which the first prefix_block_count[q] are read; entries 48 onward name the units of its SSM state, all read. Unit u belongs to owner u // 16. Over the read entries of the requests 2 r to 2 r + 1 of one replica r, no owner is named more than 2 times, and in every draw some owner is named exactly 2 times by some replica.
All inputs are finite; a program needn't handle non-finite values.
Results may differ from a plain program's by a relative error of at most 0.0075.
Values may be sent and summed in bfloat16 or wider, within the bound.
A program may use at most 64 MiB of HBM per device.

v0:
```python
import math

import jax
import jax.numpy as jnp
from jax import lax
from jax.sharding import PartitionSpec as P

HEAD_WIDTH = 128
MAMBA_HEADS = 128
MAMBA_HEAD_WIDTH = 64
STATE_WIDTH = 256
BLOCK_TOKENS = 128
MAX_PREFIX_BLOCK = 48
SUFFIX_TOKENS = 128


tile_blocks = 8


def attend(query_rows, suffix_keys, suffix_values, prefix_units, blocks_used, scaling):
    row_count = query_rows.shape[1]
    suffix_len = suffix_keys.shape[1]
    row_position = jnp.arange(row_count, dtype=jnp.int32) % suffix_len
    key_position = jnp.arange(suffix_len, dtype=jnp.int32)
    logits = (
        jnp.einsum("krd,ksd->krs", query_rows, suffix_keys, preferred_element_type=jnp.float32)
        * scaling
    )
    logits = jnp.where(key_position[None, None, :] <= row_position[None, :, None], logits, -1e30)
    row_top = jnp.max(logits, axis=-1)
    weights = jnp.exp(logits - row_top[..., None])
    totals = jnp.sum(weights, axis=-1)
    summed = jnp.einsum(
        "krs,ksd->krd",
        weights.astype(jnp.bfloat16),
        suffix_values,
        preferred_element_type=jnp.float32,
    )
    tile_count = prefix_units.shape[0] // tile_blocks
    tiles = prefix_units.reshape((tile_count, tile_blocks) + prefix_units.shape[1:])
    first_blocks = jnp.arange(tile_count, dtype=jnp.int32) * tile_blocks

    def advance(carry, tile_item):
        row_top, totals, summed = carry
        key_tile, first_block = tile_item
        tile_logits = (
            jnp.einsum(
                "krd,bksd->krbs", query_rows, key_tile[:, :, 0], preferred_element_type=jnp.float32
            )
            * scaling
        )
        block_number = first_block + jnp.arange(tile_blocks, dtype=jnp.int32)
        tile_logits = jnp.where(
            (block_number < blocks_used)[None, None, :, None], tile_logits, -1e30
        )
        new_top = jnp.maximum(row_top, jnp.max(tile_logits, axis=(2, 3)))
        fading = jnp.exp(row_top - new_top)
        tile_weights = jnp.exp(tile_logits - new_top[:, :, None, None])
        totals = totals * fading + jnp.sum(tile_weights, axis=(2, 3))
        summed = summed * fading[..., None] + jnp.einsum(
            "krbs,bksd->krd",
            tile_weights.astype(jnp.bfloat16),
            key_tile[:, :, 1],
            preferred_element_type=jnp.float32,
        )
        return ((new_top, totals, summed), None)

    (row_top, totals, summed), unused = lax.scan(
        advance, (row_top, totals, summed), (tiles, first_blocks)
    )
    return summed / totals[..., None]


def mamba_block(
    input_arrays, gate_matrix, b_rows, c_rows, deltas, decay_log, skip_gain, state_words
):
    highest = lax.Precision.HIGHEST
    suffix_len, device_heads = deltas.shape
    token_index = jnp.arange(suffix_len, dtype=jnp.int32)
    opening_state = state_words.astype(jnp.float32)
    running = jnp.cumsum(deltas * (-jnp.exp(decay_log))[None, :], axis=0)
    input_head_rows = input_arrays.astype(jnp.float32).reshape(suffix_len, device_heads, -1)
    products = jnp.dot(c_rows, b_rows.T, preferred_element_type=jnp.float32)
    causal = token_index[:, None] >= token_index[None, :]
    log_gaps = jnp.where(causal[None], running.T[:, :, None] - running.T[:, None, :], -1e30)
    kernel = jnp.exp(log_gaps) * products[None] * deltas.T[:, None, :]
    local_part = jnp.einsum("hts,shp->thp", kernel, input_head_rows, precision=highest)
    carried = jnp.exp(running)[:, :, None] * jnp.einsum(
        "tn,hpn->thp", c_rows, state_words, preferred_element_type=jnp.float32
    )
    output_arrays = local_part + carried + skip_gain[None, :, None] * input_head_rows
    tail_weight = jnp.exp(running[-1][None, :] - running) * deltas
    closing_state = jnp.exp(running[-1])[:, None, None] * opening_state + jnp.einsum(
        "shp,sn->hpn",
        tail_weight[:, :, None] * input_head_rows,
        b_rows.astype(jnp.float32),
        precision=highest,
    )
    gated_output = output_arrays.reshape(suffix_len, -1) * jax.nn.silu(
        gate_matrix.astype(jnp.float32)
    )
    return (gated_output, closing_state)


def body(
    queries,
    suffix_key_rows,
    suffix_value_rows,
    mamba_input,
    mamba_gate,
    input_projection,
    output_projection,
    step_lengths,
    decay_log,
    skip_gain,
    gated_norm_gain,
    cache_store,
    request_units,
    prefix_block_count,
):
    rep_count = lax.axis_size("rep")
    replica = lax.axis_index("rep")
    units_local = cache_store.shape[0]
    kv_local = cache_store.shape[1]
    per_request = request_units.shape[1]
    request_count = queries.shape[0] // SUFFIX_TOKENS
    positions = request_count * per_request
    capacity = -(-positions // rep_count)
    device_heads = step_lengths.shape[1]
    group_size = queries.shape[1] // (kv_local * HEAD_WIDTH)
    table = request_units.reshape(rep_count, positions)
    column = jnp.arange(per_request, dtype=jnp.int32)
    live_slot = (
        (column[None, :] < prefix_block_count[:, None]) | (column[None, :] >= MAX_PREFIX_BLOCK)
    ).reshape(rep_count, positions)
    owners = table // units_local
    slot_local = table % units_local
    ordinal = jnp.arange(positions, dtype=jnp.int32)
    earlier = (
        (owners[:, :, None] == owners[:, None, :])
        & live_slot[:, None, :]
        & (ordinal[None, None, :] < ordinal[None, :, None])
    )
    ranking = jnp.sum(earlier.astype(jnp.int32), axis=2)
    slot_number = jnp.arange(capacity, dtype=jnp.int32)
    picked = (
        (owners[:, None, :] == replica)
        & live_slot[:, None, :]
        & (ranking[:, None, :] == slot_number[None, :, None])
    )
    chosen = jnp.sum(jnp.where(picked, slot_local[:, None, :], 0), axis=2)
    filled = jnp.any(picked, axis=2)
    outgoing = cache_store[chosen]
    outgoing = jnp.where(filled[:, :, None, None, None, None], outgoing, jnp.zeros_like(outgoing))
    arrived = lax.all_to_all(outgoing, "rep", split_axis=0, concat_axis=0, tiled=True)
    arrived = arrived.reshape((rep_count * capacity,) + cache_store.shape[1:])
    own_owners = lax.dynamic_index_in_dim(owners, replica, 0, keepdims=False)
    own_ranks = lax.dynamic_index_in_dim(ranking, replica, 0, keepdims=False)
    fetched = arrived[own_owners * capacity + own_ranks].reshape(
        (request_count, per_request) + cache_store.shape[1:]
    )
    own_blocks = lax.dynamic_slice_in_dim(
        prefix_block_count, replica * request_count, request_count
    )
    scaling = 1.0 / math.sqrt(HEAD_WIDTH)
    attention_rows = []
    gated_rows = []
    square_rows = []
    state_rows = []
    for request in range(request_count):
        token_span = slice(request * SUFFIX_TOKENS, (request + 1) * SUFFIX_TOKENS)
        query_rows = (
            queries[token_span]
            .reshape(SUFFIX_TOKENS, kv_local, group_size, HEAD_WIDTH)
            .transpose(1, 2, 0, 3)
            .reshape(kv_local, group_size * SUFFIX_TOKENS, HEAD_WIDTH)
        )
        suffix_keys = (
            suffix_key_rows[token_span]
            .reshape(SUFFIX_TOKENS, kv_local, HEAD_WIDTH)
            .transpose(1, 0, 2)
        )
        suffix_values = (
            suffix_value_rows[token_span]
            .reshape(SUFFIX_TOKENS, kv_local, HEAD_WIDTH)
            .transpose(1, 0, 2)
        )
        blended = attend(
            query_rows,
            suffix_keys,
            suffix_values,
            fetched[request, :MAX_PREFIX_BLOCK],
            own_blocks[request],
            scaling,
        )
        attention_rows.append(
            blended.reshape(kv_local, group_size, SUFFIX_TOKENS, HEAD_WIDTH)
            .transpose(2, 0, 1, 3)
            .reshape(SUFFIX_TOKENS, kv_local * group_size * HEAD_WIDTH)
            .astype(jnp.bfloat16)
        )
        state_words = (
            fetched[request, MAX_PREFIX_BLOCK:]
            .reshape(per_request - MAX_PREFIX_BLOCK, kv_local, 2 * BLOCK_TOKENS * HEAD_WIDTH)
            .transpose(1, 0, 2)
            .reshape(device_heads, MAMBA_HEAD_WIDTH, STATE_WIDTH)
        )
        gated_output, closing_state = mamba_block(
            mamba_input[token_span],
            mamba_gate[token_span],
            input_projection[token_span],
            output_projection[token_span],
            step_lengths[token_span],
            decay_log,
            skip_gain,
            state_words,
        )
        gated_rows.append(gated_output)
        square_rows.append(jnp.sum(gated_output * gated_output, axis=1))
        state_rows.append(closing_state.astype(jnp.bfloat16))
    gated_all = jnp.concatenate(gated_rows, axis=0)
    square_sums = jnp.concatenate(square_rows, axis=0)
    total_sums = lax.psum(square_sums, "tp")
    inverse_norm = lax.rsqrt(total_sums / (MAMBA_HEADS * MAMBA_HEAD_WIDTH) + 1e-05)
    mamba_out = (gated_all * inverse_norm[:, None] * gated_norm_gain[None, :]).astype(jnp.bfloat16)
    attn_out = jnp.concatenate(attention_rows, axis=0)
    final_state = jnp.stack(state_rows, axis=0)
    return (attn_out, mamba_out, final_state)


def solution(mesh):
    placed = (
        P("rep", "tp"),
        P("rep", "tp"),
        P("rep", "tp"),
        P("rep", "tp"),
        P("rep", "tp"),
        P("rep", None),
        P("rep", None),
        P("rep", "tp"),
        P("tp"),
        P("tp"),
        P("tp"),
        P("rep", "tp", None, None, None),
        P(),
        P(),
    )
    return jax.shard_map(
        body,
        mesh=mesh,
        in_specs=placed,
        out_specs=(P("rep", "tp"), P("rep", "tp"), P("rep", "tp", None, None)),
        check_vma=False,
    )
```

profile of v0, /device:TPU:1, one launch (start us, length us, event | category | flops | bytes accessed | tf_op | source)
XLA Modules:
  0.0 335.5 jit_solution(14977123458681908447)
XLA Ops:
  3.0 2.5 convert_reduce_fusion
  6.1 6.5 %gather_fusion = bf16[128,2,128,128]{3,2,1,0:T(8,128)(2,1)} fusion(bf16[16,2,128,128]{3,2,1,0:T(8,128)(2,1)S(1)} %bitcast.222, s32[1024]{0:T(1024)S(1)} %pad_clamp_fusion.1), kind=kCustom, calls=%fused_computation | custom fusion | bytes 16777728 | tf_op jit(solution)/shard_map/gather | solution.py:153
  12.6 7.2 %broadcast_select_fusion = bf16[64,2,1,2,128,128]{5,4,3,1,2,0:T(8,128)(2,1)} fusion(bf16[64,2,1,2,128,128]{5,4,3,1,2,0:T(8,128)(2,1)} %bitcast.223, pred[64,2]{1,0:T(8,128)(4,1)S(1)} %copy.96), kind=kLoop, calls=%fused_computation.48 | loop fusion | flops 4194304 | bytes 16777344 | tf_op jit(solution)/shard_map/jit(_where)/select_n | solution.py:154
  19.8 12.1 %all-to-all-start = ((bf16[64,2,1,2,128,128]{5,4,3,1,2,0:T(8,128)(2,1)}), bf16[64,2,1,2,128,128]{5,4,3,1,2,0:T(8,128)(2,1)}, u32[]{:S(2)}, u32[]{:S(2)}) async-start(bf16[64,2,1,2,128,128]{5,4,3,1,2,0:T(8,128)(2,1)} %broadcast_select_fusion), calls=%async_computation | async-start | bytes 16777216 | tf_op jit(solution)/shard_map/all_to_all | solution.py:155
  44.8 173.0 %all-to-all-done = bf16[64,2,1,2,128,128]{5,4,3,1,2,0:T(8,128)(2,1)} async-done(((bf16[64,2,1,2,128,128]{5,4,3,1,2,0:T(8,128)(2,1)}), bf16[64,2,1,2,128,128]{5,4,3,1,2,0:T(8,128)(2,1)}, u32[]{:S(2)}, u32[]{:S(2)}) %all-to-all-start) | async-done | bytes 8388640 | tf_op jit(solution)/shard_map/all_to_all | solution.py:155
  217.7 9.5 %gather_fusion.1 = bf16[112,2,128,128]{3,2,1,0:T(8,128)(2,1)} fusion(bf16[128,2,128,128]{3,2,1,0:T(8,128)(2,1)} %bitcast.35, s32[1024]{0:T(1024)S(1)} %pad_clamp_fusion), kind=kCustom, calls=%fused_computation.1 | custom fusion | bytes 14680512 | tf_op jit(solution)/shard_map/gather | solution.py:159
  227.3 1.3 fusion.114
  228.5 8.1 %fusion.115 = (bf16[1,48,1,2,128,128]{5,4,3,1,2,0:T(8,128)(2,1)}, bf16[1,48,1,2,128,128]{5,4,3,1,2,0:T(8,128)(2,1)}) fusion(bf16[2,56,1,2,128,128]{5,4,3,1,2,0:T(8,128)(2,1)} %bitcast.225), kind=kLoop, calls=%fused_computation.194 | loop fusion | bytes 12582912 | tf_op jit(solution)/shard_map/slice | solution.py:192
  238.0 3.0 fusion.35
  241.0 1.3 copy.109
  243.4 2.1 fusion.33
  245.5 1.2 copy.116
  246.8 2.3 multiply_reduce_fusion.1
  249.1 19.4 %psum.7 = f32[256]{0:T(256)S(1)} all-reduce(f32[256]{0:T(256)S(1)} %pad_maximum_fusion.2), channel_id=1, replica_groups=mesh['rep'=64,'tp'=8] {'tp'}, use_global_device_ids=true, to_apply=%region_19.20 | all-reduce | flops 256 | bytes 2048 | tf_op jit(solution)/shard_map/psum | solution.py:223
  268.6 32.8 %while.28 = (s32[]{:T(128)}, f32[1,512]{1,0:T(1,128)S(1)}, f32[1,512]{1,0:T(1,128)S(1)}, f32[1,512,128]{2,1,0:T(8,128)}, s32[6]{0:T(128)S(1)}, /*index=5*/s32[]{...) while((s32[]{:T(128)}, f32[1,512]{1,0:T(1,128)S(1)}, ...), condition=%wide.region_8.9_spmd, body=%wide.region_5.8_spmd.sunk | while | flops 274334720 | bytes 10651321 | solution.py:68
  269.2 1.3 add_compare_fusion.4
  274.7 1.3 add_compare_fusion.4
  275.9 1.1 copy_bitcast_fusion.6
  280.1 1.3 add_compare_fusion.4
  285.6 1.3 add_compare_fusion.4
  291.0 1.3 add_compare_fusion.4
  292.3 1.1 copy_bitcast_fusion.6
  296.5 1.3 add_compare_fusion.4
  297.8 1.1 copy_bitcast_fusion.6
  301.3 1.1 divide_convert_fusion.1
  302.6 28.6 %while.29 = (s32[]{:T(128)}, f32[1,512]{1,0:T(1,128)S(1)}, f32[1,512]{1,0:T(1,128)S(1)}, f32[1,512,128]{2,1,0:T(8,128)S(1)}, s32[6]{0:T(128)S(1)}, /*index=5*/s3...) while((s32[]{:T(128)}, f32[1,512]{1,0:T(1,128)S(1)}, ...), condition=%wide.region_14.15_spmd, body=%wide.region_11.14_spmd.sunk | while | flops 274334720 | bytes 8554113 | solution.py:68
  303.2 1.3 add_compare_fusion.5
  308.0 1.3 add_compare_fusion.5
  312.7 1.3 add_compare_fusion.5
  317.5 1.3 add_compare_fusion.5
  322.2 1.3 add_compare_fusion.5
  327.0 1.3 add_compare_fusion.5
  (252 shorter events, 64.0 us)
Async XLA Ops:
  0.6 5.5 %copy-start = (bf16[16,1,2,128,128]{4,3,2,1,0:T(8,128)(2,1)S(1)}, bf16[16,1,2,128,128]{4,3,2,1,0:T(8,128)(2,1)}, u32[]{:S(2)}) copy-start(bf16[16,1,2,128,128]{4,3,2,1,0:T(8,128)(2,1)} %param.29) | copy-start | bytes 3145732
  19.8 12.2 %copy-start.19 = (f32[256,16]{0,1:T(8,128)S(1)}, f32[256,16]{0,1:T(8,128)}, u32[]{:S(2)}) copy-start(f32[256,16]{0,1:T(8,128)} %param.25) | copy-start | bytes 49156
  19.8 13.0 %copy-start.28 = (f32[16]{0:T(128)S(1)}, f32[16]{0:T(128)}, u32[]{:S(2)}) copy-start(f32[16]{0:T(128)} %param.26) | copy-start | bytes 196
  19.8 13.9 %copy-start.13 = (bf16[256,1024]{1,0:T(8,128)(2,1)S(1)}, bf16[256,1024]{1,0:T(8,128)(2,1)}, u32[]{:S(2)}) copy-start(bf16[256,1024]{1,0:T(8,128)(2,1)} %param.21) | copy-start | bytes 1572868
  19.8 198.0 %all-to-all-start = ((bf16[64,2,1,2,128,128]{5,4,3,1,2,0:T(8,128)(2,1)}), bf16[64,2,1,2,128,128]{5,4,3,1,2,0:T(8,128)(2,1)}, u32[]{:S(2)}, u32[]{:S(2)}) async-start(bf16[64,2,1,2,128,128]{5,4,3,1,2,0:T(8,128)(2,1)} %broadcast_select_fusion), calls=%async_computation | async-start | bytes 16777216 | tf_op jit(solution)/shard_map/all_to_all | solution.py:155
  31.9 5.7 %copy-start.26 = (s32[128]{0:T(128)S(1)}, s32[128]{0:T(128)}, u32[]{:S(2)}) copy-start(s32[128]{0:T(128)} %param.31) | copy-start | bytes 1540
  32.0 5.8 %copy-start.14 = (bf16[256,512]{1,0:T(8,128)(2,1)S(1)}, bf16[256,512]{1,0:T(8,128)(2,1)}, u32[]{:S(2)}) copy-start(bf16[256,512]{1,0:T(8,128)(2,1)} %param.18) | copy-start | bytes 786436
  33.7 6.0 %copy-start.27 = (bf16[256,128]{1,0:T(8,128)(2,1)S(1)}, bf16[256,128]{1,0:T(8,128)(2,1)}, u32[]{:S(2)}) copy-start(bf16[256,128]{1,0:T(8,128)(2,1)} %param.19) | copy-start | bytes 196612
  33.9 209.4 %copy-start.3 = (bf16[128,1024]{0,1:T(8,128)(2,1)}, bf16[128,1024]{0,1:T(8,128)(2,1)S(1)}, u32[]{:S(2)}) copy-start(bf16[128,1024]{0,1:T(8,128)(2,1)S(1)} %copy.114) | copy-start | bytes 786436
  34.1 6.1 %copy-start.15 = (bf16[256,128]{1,0:T(8,128)(2,1)S(1)}, bf16[256,128]{1,0:T(8,128)(2,1)}, u32[]{:S(2)}) copy-start(bf16[256,128]{1,0:T(8,128)(2,1)} %param.20) | copy-start | bytes 196612
  35.0 203.0 %copy-start.5 = (bf16[128,1024]{0,1:T(8,128)(2,1)}, bf16[128,1024]{0,1:T(8,128)(2,1)S(1)}, u32[]{:S(2)}) copy-start(bf16[128,1024]{0,1:T(8,128)(2,1)S(1)} %copy.107) | copy-start | bytes 786436
  37.0 6.2 %copy-start.10 = (bf16[256,256]{1,0:T(8,128)(2,1)S(1)}, bf16[256,256]{1,0:T(8,128)(2,1)}, u32[]{:S(2)}) copy-start(bf16[256,256]{1,0:T(8,128)(2,1)} %param.24) | copy-start | bytes 393220
  37.0 6.2 %copy-start.11 = (bf16[256,256]{1,0:T(8,128)(2,1)S(1)}, bf16[256,256]{1,0:T(8,128)(2,1)}, u32[]{:S(2)}) copy-start(bf16[256,256]{1,0:T(8,128)(2,1)} %param.23) | copy-start | bytes 393220
  241.0 2.3 copy-start.16
  241.0 2.4 copy-start.20
  241.0 2.4 copy-start.21
  241.0 2.4 copy-start.22
  241.0 2.4 copy-start.29
  245.5 23.0 %copy-start.30 = (s32[6]{0:T(128)S(1)}, s32[6]{0:T(128)}, u32[]{:S(2)}) copy-start(s32[6]{0:T(128)} %iota_multiply_fusion) | copy-start | bytes 76
  268.5 34.0 %copy-start.7 = (f32[1,512,128]{2,1,0:T(8,128)S(1)}, f32[1,512,128]{2,1,0:T(8,128)}, u32[]{:S(2)}) copy-start(f32[1,512,128]{2,1,0:T(8,128)} %convolution_bitcast_fusion.6) | copy-start | bytes 786436
  277.0 1.0 copy-start.8
  288.0 1.0 copy-start.8
  298.9 1.0 copy-start.8
  302.5 28.9 %copy-start.4 = (bf16[128,1024]{0,1:T(8,128)(2,1)S(1)}, bf16[128,1024]{0,1:T(8,128)(2,1)}, u32[]{:S(2)}) copy-start(bf16[128,1024]{0,1:T(8,128)(2,1)} %copy-done.3) | copy-start | bytes 786436
  302.5 28.9 %copy-start.12 = (bf16[256,256]{1,0:T(8,128)(2,1)S(1)}, bf16[256,256]{1,0:T(8,128)(2,1)}, u32[]{:S(2)}) copy-start(bf16[256,256]{1,0:T(8,128)(2,1)} %param.23) | copy-start | bytes 393220
  302.5 28.9 %copy-start.17 = (f32[128,16]{0,1:T(8,128)S(1)}, f32[128,16]{0,1:T(8,128)}, u32[]{:S(2)}) copy-start(f32[128,16]{0,1:T(8,128)} %copy.118) | copy-start | bytes 24580
  302.6 28.9 %copy-start.25 = (f32[16]{0:T(128)S(1)}, f32[16]{0:T(128)}, u32[]{:S(2)}) copy-start(f32[16]{0:T(128)} %fusion.111) | copy-start | bytes 196
  302.6 29.5 %copy-start.18 = (f32[128,16]{0,1:T(8,128)S(1)}, f32[128,16]{0,1:T(8,128)}, u32[]{:S(2)}) copy-start(f32[128,16]{0,1:T(8,128)} %copy.117) | copy-start | bytes 24580
  302.6 29.5 %copy-start.24 = (f32[16]{0:T(128)S(1)}, f32[16]{0:T(128)}, u32[]{:S(2)}) copy-start(f32[16]{0:T(128)} %fusion.110) | copy-start | bytes 196
  332.1 2.4 copy-start.1
  332.1 2.4 copy-start.2
  332.1 2.4 copy-start.23
  (10 other events, 8.2 us)
where the time goes:
time: 338 us; the launch traced here: 336 us
  waiting for transfers between devices  173 us (51%)
  local copies, waits for them, and re-layouts  62.9 us (19%)
  other arithmetic  40.2 us (12%)
  matrix products  26 us (8%)
  blocking collectives  19.4 us (6%)
  starting transfers between devices  12.1 us (4%)
    all_to_all x1, waiting for transfers between devices, body(): lax.all_to_all(outgoing, 'rep', split_axis=0, concat_axis=0, tiled=True)  173 us
    psum x1, blocking collectives, body(): total_sums = lax.psum(square_sums, 'tp')  19.4 us
    lt x12, other arithmetic, advance(): block_number < blocks_used  15.7 us
    squeeze x12, local copies, waits for them, and re-layouts, attend(): lax.scan(advance, (row_top, totals, summed), (tiles, first_blocks))  13 us
    all_to_all x1, starting transfers between devices, body(): lax.all_to_all(outgoing, 'rep', split_axis=0, concat_axis=0, tiled=True)  12.1 us
    gather x1, local copies, waits for them, and re-layouts, body(): arrived[own_owners * capacity + own_ranks]  9.52 us
    dot_general x12, matrix products, advance(): jnp.einsum('krbs,bksd->krd', tile_weights.astype(jnp.bfloat16), key_tile[...  8.51 us
    slice x1, local copies, waits for them, and re-layouts, body(): fetched[request, :MAX_PREFIX_BLOCK]  8.08 us
  transfers between devices with their start and end apart: 1, of which 1 were waited for; matrix products, arithmetic and copies ran while one was open for 4% of the time, Pallas kernels for 0%

commit v1 on v0

v1 whole, which is shorter than its diff:
```python
import math

import jax
import jax.numpy as jnp
from jax import lax
from jax.experimental import pallas as pl
from jax.experimental.pallas import tpu as pltpu
from jax.sharding import PartitionSpec as P

MESH = pl.DeviceIdType.MESH
HEAD_WIDTH = 128
MAMBA_COLUMNS = 8192
MAX_PREFIX_BLOCK = 48
PER_REQUEST = 56
POSITIONS = 112
TOKENS = 128
XN, YN, CN, ZN = 4, 8, 2, 8
UNITS = 16
GROUP = 8
GROUPS = MAX_PREFIX_BLOCK // GROUP
ROWS = 512
PAIRS = 8
NEG = -1e30
HIGHEST = lax.Precision.HIGHEST
SCALING = 1.0 / math.sqrt(HEAD_WIDTH)
PARTNERS = [(dx, dc) for dx in range(XN) for dc in range(CN)]


def dot_nt(a, b, precision=None):
    return lax.dot_general(
        a, b, (((1,), (1,)), ((), ())), precision=precision, preferred_element_type=jnp.float32
    )


def dot_tn(a, b, precision=None):
    return lax.dot_general(
        a, b, (((0,), (0,)), ((), ())), precision=precision, preferred_element_type=jnp.float32
    )


def dot_nn(a, b, precision=None):
    return jnp.dot(a, b, precision=precision, preferred_element_type=jnp.float32)


def kernel(
    send_index, position_index, counts,
    queries, suffix_keys, suffix_values, mamba_x, mamba_gate, b_rows, c_rows,
    steps, decay_log, skip_lanes, norm_gain, cache,
    attn_out, mamba_out, final_state,
    yk, yv, pick, xk, xv, kin, vin, probs, suffix_probs, scores, query_scr,
    top, total, group_top, out_acc, products, run_col, run_row, step_row, local_y,
    closing, square_out, square_in,
    y_send, y_recv, x_send, x_recv, z_send, z_recv,
):
    rep = lax.axis_index("rep")
    tp = lax.axis_index("tp")
    x, y, c = rep // 16, (rep // 2) % YN, rep % 2

    def device(dx, dy, dc):
        return (((x + dx) % XN * YN + (y + dy) % YN) * CN + (c + dc) % CN, tp)

    barrier = pltpu.get_barrier_semaphore()
    for dx, dc in PARTNERS[1:]:
        pl.semaphore_signal(barrier, 1, device_id=device(dx, 0, dc), device_id_type=MESH)
    for dy in (1, YN - 1):
        pl.semaphore_signal(barrier, 1, device_id=device(0, dy, 0), device_id_type=MESH)
    for dz in range(1, ZN):
        pl.semaphore_signal(barrier, 1, device_id=(rep, (tp + dz) % ZN), device_id_type=MESH)
    pl.semaphore_wait(barrier, len(PARTNERS) - 1 + 2 + ZN - 1)

    ybufs, xbufs, inbufs = (yk, yv), (xk, xv), (kin, vin)

    def y_copy(phase, direction, src, ss):
        distance, half = ss // 2 + 1, ss % 2
        row = distance - 1 if direction == 0 else YN - 1 - distance
        half = half if direction == 0 else 1 - half
        dst = ybufs[phase].at[row, pl.ds(half * 8, 8)]
        slot = (direction * 2 + phase) * 7 + ss
        return pltpu.make_async_remote_copy(
            src_ref=dst if src is None else src,
            dst_ref=dst,
            send_sem=y_send.at[slot],
            recv_sem=y_recv.at[slot],
            device_id=device(0, 1 if direction == 0 else YN - 1, 0),
            device_id_type=MESH,
        )

    def y_own(phase, direction, ss):
        half = ss if direction == 0 else 1 - ss
        return y_copy(phase, direction, cache.at[pl.ds(half * 8, 8), phase], ss)

    def y_forward(phase, direction, ss):
        distance, half = ss // 2 + 1, ss % 2
        row = distance - 1 if direction == 0 else YN - 1 - distance
        half = half if direction == 0 else 1 - half
        return y_copy(phase, direction, ybufs[phase].at[row, pl.ds(half * 8, 8)], ss + 2)

    def x_copy(phase, dy, j):
        dx, dc = PARTNERS[j]
        slot = (phase * YN + dy) * 7 + j - 1
        return pltpu.make_async_remote_copy(
            src_ref=xbufs[phase].at[dy, j - 1],
            dst_ref=inbufs[phase].at[pl.ds((j * YN + dy) * 2, 2)],
            send_sem=x_send.at[slot],
            recv_sem=x_recv.at[slot],
            device_id=device(dx, 0, dc),
            device_id_type=MESH,
        )

    def send_chosen(phase, dy):
        for j, (dx, dc) in enumerate(PARTNERS):
            target = ((x + dx) % XN) * CN + (c + dc) % CN
            for s in range(2):
                unit = send_index[(dy * 8 + target) * 2 + s]
                if j == 0:
                    inbufs[phase][dy * 2 + s] = pick[unit]
                else:
                    xbufs[phase][dy, j - 1, s] = pick[unit]
            if j > 0:
                x_copy(phase, dy, j).start()

    for direction in (0, 1):
        for ss in (0, 1):
            y_own(0, direction, ss).start()
    for phase in (0, 1):
        pick[...] = cache[:, phase]
        send_chosen(phase, 0)

    lane = lax.broadcasted_iota(jnp.int32, (TOKENS, 128), 1)
    row = lax.broadcasted_iota(jnp.int32, (TOKENS, 128), 0)
    low_half = lane < 64
    lane16 = lax.broadcasted_iota(jnp.int32, (TOKENS, 16), 1)
    causal = row >= lane
    rates = -jnp.exp(decay_log[...])

    def prepare(q, carry):
        rows = pl.ds(pl.multiple_of(q * TOKENS, TOKENS), TOKENS)
        for h in range(4):
            query_scr[q, pl.ds(h * TOKENS, TOKENS)] = queries[rows, pl.ds(h * 128, 128)]
        delta = steps[rows, :]
        lower = (row >= lane).astype(jnp.float32)
        upper = (row <= lane).astype(jnp.float32)
        unit = (row == lane).astype(jnp.float32)
        run_col[q] = dot_nn(lower, delta * rates, HIGHEST)
        run_row[q] = dot_tn(delta * rates, upper, HIGHEST)
        step_row[q] = dot_tn(delta, unit, HIGHEST)
        products[q] = jnp.where(causal, dot_nt(c_rows[rows, :], b_rows[rows, :]), 0.0)
        keys = suffix_keys[rows, :]
        for h in range(4):
            part = pl.ds(h * TOKENS, TOKENS)
            s = dot_nt(query_scr[q, part], keys) * SCALING
            s = jnp.where(causal, s, NEG)
            m = jnp.broadcast_to(jnp.max(s, axis=1, keepdims=True), (TOKENS, 128))
            p = jnp.exp(s - m)
            top[q, part] = m
            group_top[q * (GROUPS + 1) + GROUPS, part] = m
            total[q, part] = p
            suffix_probs[q, part] = p.astype(jnp.bfloat16)
        return carry

    lax.fori_loop(0, 2, prepare, 0)

    def column(ref, q_rows, h):
        return jnp.sum(jnp.where(lane16 == h, ref[q_rows], 0.0), axis=1, keepdims=True)

    def mamba_pair(i, carry):
        q, p = i // PAIRS, i % PAIRS
        rows = pl.ds(pl.multiple_of(q * TOKENS, TOKENS), TOKENS)
        lanes = pl.ds(pl.multiple_of(p * 128, 128), 128)
        xs = mamba_x[rows, lanes]
        parts, tails = [], []
        run = run_col[q]
        delta = steps[rows, :]
        for e in (0, 1):
            h = 2 * p + e
            rc = jnp.sum(jnp.where(lane16 == h, run, 0.0), axis=1, keepdims=True)
            dc = jnp.sum(jnp.where(lane16 == h, delta, 0.0), axis=1, keepdims=True)
            rr = run_row[q, pl.ds(h, 1)]
            dr = step_row[q, pl.ds(h, 1)]
            gaps = jnp.where(causal, rc - rr, NEG)
            mix = jnp.exp(gaps) * products[q] * dr
            parts.append(dot_nn(mix.astype(jnp.bfloat16), xs))
            tails.append(jnp.exp(rc[TOKENS - 1 : TOKENS] - rc) * dc)
        xf = xs.astype(jnp.float32)
        local_y[rows, lanes] = jnp.where(low_half, parts[0], parts[1]) + skip_lanes[:, lanes] * xf
        weighted = (xf * jnp.where(low_half, tails[0], tails[1])).astype(jnp.bfloat16)
        closing[i] = dot_tn(weighted, b_rows[rows, :])
        return carry

    source_row = jnp.where(row < 64, 2 * row, 2 * (row - 64) + 1)
    deal = (lane == source_row).astype(jnp.bfloat16)

    def state_head(phase):
        def step(i, carry):
            q, p = i // PAIRS, i % PAIRS
            rows = pl.ds(pl.multiple_of(q * TOKENS, TOKENS), TOKENS)
            lanes = pl.ds(pl.multiple_of(p * 128, 128), 128)
            h = 2 * p + phase
            unit = inbufs[phase][position_index[q * PER_REQUEST + MAX_PREFIX_BLOCK + p]]
            dealt = dot_nn(deal, unit)
            state = jnp.concatenate([dealt[:64], dealt[64:]], axis=1)
            rc = jnp.sum(jnp.where(lane16 == h, run_col[q], 0.0), axis=1, keepdims=True)
            blank = jnp.zeros((64, 256), jnp.bfloat16)
            sb = state.astype(jnp.bfloat16)
            both = [sb, blank] if phase == 0 else [blank, sb]
            carried = dot_nt(c_rows[rows, :], jnp.concatenate(both, axis=0))
            local_y[rows, lanes] = local_y[rows, lanes] + jnp.exp(rc) * carried
            last = jnp.exp(rc[TOKENS - 1 : TOKENS])
            final_state[q, h] = (
                last * state + closing[i, pl.ds(phase * 64, 64)]
            ).astype(jnp.bfloat16)
            return carry

        return step

    def score_group(i, carry):
        q, g = i // GROUPS, i % GROUPS
        qv = query_scr[q]
        for b in range(GROUP):
            block = g * GROUP + b
            key = kin[position_index[q * PER_REQUEST + block]]
            s = dot_nt(qv, key) * SCALING
            scores[:, pl.ds(b * 128, 128)] = jnp.where(block < counts[q], s, NEG)
        for r in range(4):
            part = pl.ds(r * TOKENS, TOKENS)
            mx = scores[part, pl.ds(0, 128)]
            for b in range(1, GROUP):
                mx = jnp.maximum(mx, scores[part, pl.ds(b * 128, 128)])
            old = top[q, part]
            m = jnp.maximum(old, jnp.max(mx, axis=1, keepdims=True))
            acc = total[q, part] * jnp.exp(old - m)
            for b in range(GROUP):
                p = jnp.exp(scores[part, pl.ds(b * 128, 128)] - m)
                acc = acc + p
                probs[i, part, pl.ds(b * 128, 128)] = p.astype(jnp.bfloat16)
            total[q, part] = acc
            top[q, part] = m
            group_top[q * (GROUPS + 1) + g, part] = m
        return carry

    def wait_in(phase):
        def step(dy, carry):
            for j in range(1, 8):
                x_copy(phase, dy, j).wait_recv()
            return carry

        lax.fori_loop(0, YN, step, 0)

    for phase in (0, 1):

        def ring_step(ss, carry, phase=phase):
            k = ss // 2 + 1
            for direction in (0, 1):
                y_copy(phase, direction, None, ss).wait_recv()

                @pl.when(ss <= 4)
                def _():
                    y_forward(phase, direction, ss).start()

                if phase == 0:

                    @pl.when(ss == 4)
                    def _():
                        y_own(1, direction, 0).start()

                    @pl.when(ss == 6)
                    def _():
                        y_own(1, direction, 1).start()

            @pl.when((ss % 2 == 1) | (ss == 6))
            def _():
                pick[...] = ybufs[phase][k - 1]
                send_chosen(phase, k)

            @pl.when(ss % 2 == 1)
            def _():
                pick[...] = ybufs[phase][YN - 1 - k]
                send_chosen(phase, YN - k)

            if phase == 0:
                lax.fori_loop(ss * 16 // 7, (ss + 1) * 16 // 7, mamba_pair, 0)
            else:

                @pl.when(ss == 0)
                def _():
                    wait_in(0)
                    lax.fori_loop(0, 16, state_head(0), 0)

                @pl.when(ss > 0)
                def _():
                    lax.fori_loop(ss * 2 - 2, ss * 2, score_group, 0)

            return carry

        lax.fori_loop(0, 7, ring_step, 0)

    for q in range(2):
        shrink = jnp.exp(group_top[q * (GROUPS + 1) + GROUPS] - top[q])
        out_acc[q] = shrink * dot_nn(suffix_probs[q], suffix_values[pl.ds(q * TOKENS, TOKENS), :])

    wait_in(1)
    lax.fori_loop(0, 16, state_head(1), 0)

    ones8 = jnp.ones((8, 128), jnp.float32)
    for q in range(2):
        rows = pl.ds(q * TOKENS, TOKENS)

        def gate_pair(p, squares, rows=rows):
            lanes = pl.ds(pl.multiple_of(p * 128, 128), 128)
            gate = mamba_gate[rows, lanes].astype(jnp.float32)
            gated = local_y[rows, lanes] * (gate / (1.0 + jnp.exp(-gate)))
            local_y[rows, lanes] = gated
            return squares + gated * gated

        squares = lax.fori_loop(0, PAIRS, gate_pair, jnp.zeros((TOKENS, 128), jnp.float32))
        square_out[q] = dot_nt(ones8, squares, HIGHEST)

    def z_copy(dz):
        return pltpu.make_async_remote_copy(
            src_ref=square_out,
            dst_ref=square_in.at[dz - 1],
            send_sem=z_send.at[dz - 1],
            recv_sem=z_recv.at[dz - 1],
            device_id=(rep, (tp + dz) % ZN),
            device_id_type=MESH,
        )

    for dz in range(1, ZN):
        z_copy(dz).start()

    def blend_group(i, carry):
        q, g = i // GROUPS, i % GROUPS
        values = [vin[position_index[q * PER_REQUEST + g * GROUP + b]] for b in range(GROUP)]
        blended = dot_nn(probs[i], jnp.concatenate(values, axis=0))
        out_acc[q] = out_acc[q] + jnp.exp(group_top[q * (GROUPS + 1) + g] - top[q]) * blended
        return carry

    lax.fori_loop(0, 2 * GROUPS, blend_group, 0)
    for q in range(2):
        for h in range(4):
            part = pl.ds(h * TOKENS, TOKENS)
            weight = jnp.sum(total[q, part], axis=1, keepdims=True)
            attn_out[pl.ds(q * TOKENS, TOKENS), pl.ds(h * 128, 128)] = (
                out_acc[q, part] / weight
            ).astype(jnp.bfloat16)

    for dz in range(1, ZN):
        z_copy(dz).wait_recv()
    unit = (row == lane).astype(jnp.float32)
    ones = jnp.ones((128, 128), jnp.float32)
    for q in range(2):
        sums = square_out[q]
        for dz in range(1, ZN):
            sums = sums + square_in[dz - 1, q]
        scale_row = lax.rsqrt(sums[0:1] / MAMBA_COLUMNS + 1e-05)
        scale = dot_nn(unit * scale_row, ones, HIGHEST)
        rows = pl.ds(q * TOKENS, TOKENS)

        def norm_pair(p, carry, rows=rows, scale=scale):
            lanes = pl.ds(pl.multiple_of(p * 128, 128), 128)
            mamba_out[rows, lanes] = (
                local_y[rows, lanes] * scale * norm_gain[:, lanes]
            ).astype(jnp.bfloat16)
            return carry

        lax.fori_loop(0, PAIRS, norm_pair, 0)

    def drain_y(ss, carry):
        for phase in (0, 1):
            for direction in (0, 1):
                y_copy(phase, direction, None, ss).wait_send()
        return carry

    def drain_x(dy, carry):
        for phase in (0, 1):
            for j in range(1, 8):
                x_copy(phase, dy, j).wait_send()
        return carry

    lax.fori_loop(0, 7, drain_y, 0)
    lax.fori_loop(0, YN, drain_x, 0)
    for dz in range(1, ZN):
        z_copy(dz).wait_send()


def tables(request_units, prefix_block_count):
    rep = lax.axis_index("rep")
    x, y, c = rep // 16, (rep // 2) % YN, rep % 2
    slot = jnp.arange(PER_REQUEST, dtype=jnp.int32)
    live = (slot[None, :] < prefix_block_count[:, None]) | (slot[None, :] >= MAX_PREFIX_BLOCK)
    owner = jnp.where(live, request_units // UNITS, -1).reshape(XN, YN, CN, POSITIONS)
    local = (request_units % UNITS).reshape(XN, YN, CN, POSITIONS)
    owner = lax.dynamic_index_in_dim(owner, y, 1, keepdims=False).reshape(XN * CN, POSITIONS)
    local = lax.dynamic_index_in_dim(local, y, 1, keepdims=False).reshape(XN * CN, POSITIONS)
    distance = jnp.arange(YN, dtype=jnp.int32)
    sources = (x * YN + (y - distance + YN) % YN) * CN + c
    ordinal = jnp.arange(POSITIONS, dtype=jnp.int32)
    code = ordinal[None, :] * UNITS + local
    hit = owner[None] == sources[:, None, None]
    first = jnp.min(jnp.where(hit, code[None], POSITIONS * UNITS), axis=2) % UNITS
    last = jnp.max(jnp.where(hit, code[None], 0), axis=2) % UNITS
    send_index = jnp.stack([first, last], axis=2).reshape(-1)
    own = lax.dynamic_index_in_dim(owner, x * CN + c, 0, keepdims=False)
    again = jnp.any(
        (own[:, None] == own[None, :]) & (ordinal[None, :] < ordinal[:, None]), axis=1
    ).astype(jnp.int32)
    ox, oy, oc = own // 16, (own // 2) % YN, own % 2
    j = ((x - ox + XN) % XN) * CN + (c - oc + CN) % CN
    position_index = (j * YN + (y - oy + YN) % YN) * 2 + again
    position_index = jnp.where(own >= 0, position_index, 0)
    counts = lax.dynamic_slice_in_dim(prefix_block_count, rep * 2, 2)
    return send_index, position_index, counts


def body(
    queries, suffix_key_rows, suffix_value_rows, mamba_input, mamba_gate, input_projection,
    output_projection, step_lengths, decay_log, skip_gain, gated_norm_gain, cache_store,
    request_units, prefix_block_count,
):
    send_index, position_index, counts = tables(request_units, prefix_block_count)
    bf16, f32 = jnp.bfloat16, jnp.float32
    vmem = pl.BlockSpec(memory_space=pltpu.VMEM)
    smem = pl.BlockSpec(memory_space=pltpu.SMEM)
    return pl.pallas_call(
        kernel,
        out_shape=(
            jax.ShapeDtypeStruct((256, 512), bf16),
            jax.ShapeDtypeStruct((256, 1024), bf16),
            jax.ShapeDtypeStruct((2, 16, 64, 256), bf16),
        ),
        in_specs=[smem] * 3 + [vmem] * 12,
        out_specs=[vmem] * 3,
        scratch_shapes=[
            pltpu.VMEM((7, UNITS, 128, 128), bf16),
            pltpu.VMEM((7, UNITS, 128, 128), bf16),
            pltpu.VMEM((UNITS, 128, 128), bf16),
            pltpu.VMEM((8, 7, 2, 128, 128), bf16),
            pltpu.VMEM((8, 7, 2, 128, 128), bf16),
            pltpu.VMEM((128, 128, 128), bf16),
            pltpu.VMEM((128, 128, 128), bf16),
            pltpu.VMEM((2 * GROUPS, ROWS, GROUP * 128), bf16),
            pltpu.VMEM((2, ROWS, 128), bf16),
            pltpu.VMEM((ROWS, GROUP * 128), f32),
            pltpu.VMEM((2, ROWS, 128), bf16),
            pltpu.VMEM((2, ROWS, 128), f32),
            pltpu.VMEM((2, ROWS, 128), f32),
            pltpu.VMEM((2 * (GROUPS + 1), ROWS, 128), f32),
            pltpu.VMEM((2, ROWS, 128), f32),
            pltpu.VMEM((2, 128, 128), f32),
            pltpu.VMEM((2, 128, 16), f32),
            pltpu.VMEM((2, 16, 128), f32),
            pltpu.VMEM((2, 16, 128), f32),
            pltpu.VMEM((256, 1024), f32),
            pltpu.VMEM((16, 128, 256), f32),
            pltpu.VMEM((2, 8, 128), f32),
            pltpu.VMEM((7, 2, 8, 128), f32),
            pltpu.SemaphoreType.DMA((28,)),
            pltpu.SemaphoreType.DMA((28,)),
            pltpu.SemaphoreType.DMA((112,)),
            pltpu.SemaphoreType.DMA((112,)),
            pltpu.SemaphoreType.DMA((7,)),
            pltpu.SemaphoreType.DMA((7,)),
        ],
        compiler_params=pltpu.CompilerParams(
            collective_id=0, has_side_effects=True, vmem_limit_bytes=62 << 20
        ),
    )(
        send_index, position_index, counts,
        queries, suffix_key_rows, suffix_value_rows, mamba_input, mamba_gate, input_projection,
        output_projection, step_lengths, decay_log[None], jnp.repeat(skip_gain, 64)[None],
        gated_norm_gain[None], cache_store.reshape(UNITS, 2, 128, 128),
    )


def solution(mesh):
    placed = (
        P("rep", "tp"),
        P("rep", "tp"),
        P("rep", "tp"),
        P("rep", "tp"),
        P("rep", "tp"),
        P("rep", None),
        P("rep", None),
        P("rep", "tp"),
        P("tp"),
        P("tp"),
        P("tp"),
        P("rep", "tp", None, None, None),
        P(),
        P(),
    )
    return jax.shard_map(
        body,
        mesh=mesh,
        in_specs=placed,
        out_specs=(P("rep", "tp"), P("rep", "tp"), P("rep", "tp", None, None)),
        check_vma=False,
    )
```

time: 338 us -> 146 us (0.43)
  waiting for transfers between devices: 173 us -> 0 us
  Pallas kernels: 0 us -> 134 us
  local copies, waits for them, and re-layouts: 62.9 us -> 9.25 us
  other arithmetic: 40.2 us -> 1.34 us
  matrix products: 26 us -> 0 us
  blocking collectives: 19.4 us -> 0 us
  starting transfers between devices: 12.1 us -> 0 us
    all_to_all x1 -> x0, waiting for transfers between devices: 173 us -> none  [body(): lax.all_to_all(outgoing, 'rep', split_axis=0, concat_axis=0, tiled=True)]
    pallas_call x0 -> x1, Pallas kernels: none -> 134 us  [body(): pl.pallas_call(kernel, out_shape=(jax.ShapeDtypeStruct((256, 512), bf16),...]
    dot_general x36 -> x0, matrix products: 26 us -> none  [the longest x12 8.51 us: advance(): jnp.einsum('krbs,bksd->krd', tile_weights.astype(jnp.bfloat16), key_tile[...]
    psum x1 -> x0, blocking collectives: 19.4 us -> none  [body(): total_sums = lax.psum(square_sums, 'tp')]
    gather x2 -> x0, local copies, waits for them, and re-layouts: 16 us -> none  [the longest x1 9.52 us: body(): arrived[own_owners * capacity + own_ranks]]
    lt x13 -> x0, other arithmetic: 15.7 us -> none  [the longest x12 15.7 us: advance(): block_number < blocks_used]
    squeeze x14 -> x1, local copies, waits for them, and re-layouts: 13 us -> 0.01 us  [tables(): own = lax.dynamic_index_in_dim(owner, x * CN + c, 0, keepdims=False)]
    all_to_all x1 -> x0, starting transfers between devices: 12.1 us -> none  [body(): lax.all_to_all(outgoing, 'rep', split_axis=0, concat_axis=0, tiled=True)]
  transfers between devices with their start and end apart: 1 -> 0, of which waited for: 1 -> 0; matrix products, arithmetic and copies ran while one was open for 4% -> 0% of each run, Pallas kernels for 0% -> 0%
where the time goes in v1:
time: 146 us
  Pallas kernels  134 us (92%)
  local copies, waits for them, and re-layouts  9.25 us (6%)
    pallas_call x1, Pallas kernels, body(): pl.pallas_call(kernel, out_shape=(jax.ShapeDtypeStruct((256, 512), bf16),...  134 us
    unnamed x14, local copies, waits for them, and re-layouts  6.68 us

profile of v1, /device:TPU:1, one launch (start us, length us, event | category | flops | bytes accessed | tf_op | source)
XLA Modules:
  0.0 145.6 jit_solution(4177542363339345338)
XLA Ops:
  0.7 0.0 copy-start.3
  0.7 0.0 copy-start.1
  0.7 0.6 copy-done.3
  1.3 0.7 dynamic_slice.17.counts
  2.0 0.0 copy-start.4
  2.0 0.6 copy-done.4
  2.7 0.1 broadcast_in_dim.46
  2.7 0.7 broadcast_in_dim_reshape.4.skip_lanes
  3.4 0.0 copy-done.1
  3.4 0.1 fusion.4
  3.5 0.1 copy.23
  3.6 0.1 reshape.151
  3.7 0.1 copy.24
  3.8 0.1 reshape.152
  3.9 0.2 fusion.1
  4.1 0.6 compare_select_fusion.12.position_index
  4.7 0.4 fusion.2
  5.2 0.1 copy.25
  5.3 0.0 copy-start.2
  5.3 0.7 reshape.154.send_index
  6.0 0.1 copy-done.2
  6.0 0.8 copy.26.steps
  6.8 134.2 %shard_map.157 = (bf16[256,512]{1,0:T(8,128)(2,1)}, bf16[256,1024]{1,0:T(8,128)(2,1)}, bf16[2,16,64,256]{3,2,1,0:T(8,128)(2,1)}) custom-call(s32[128]{0:T(128)} %reshape.154.send_index, s32[112]{0:T(128)} %compare_select_fusion.12.position_index, s32[2]{0:T(128)} %dynamic_slice.17.counts, bf16[256,512]{1,0:T(8,128)(2,1)} %queries.1, ...), custom_call_target="tpu_custom_call" | custom-call | tf_op jit(solution)/shard_map/pallas_call | solution.py:424
  141.0 0.0 copy-start
  141.0 1.8 %copy.30 = bf16[256,512]{1,0:T(8,128)(2,1)} copy(bf16[256,512]{1,0:T(8,128)(2,1)} %get-tuple-element.12) | data formatting | bytes 524288
  142.8 1.9 %copy.31 = bf16[256,1024]{1,0:T(8,128)(2,1)} copy(bf16[256,1024]{1,0:T(8,128)(2,1)} %get-tuple-element.13) | data formatting | bytes 1048576
  144.7 0.0 copy-done
  144.7 1.0 copy.32
  (9 shorter events, 0.1 us)
Async XLA Ops:
  0.7 0.7 copy-start.3
  0.7 2.7 %copy-start.1 = (s32[128,56]{0,1:T(8,128)S(1)}, s32[128,56]{0,1:T(8,128)}, u32[]{:S(2)}) copy-start(s32[128,56]{0,1:T(8,128)} %param.26) | copy-start | bytes 86020
  2.0 0.7 copy-start.4
  5.3 0.7 copy-start.2
  141.0 3.6 %copy-start = (bf16[2,16,64,256]{3,2,1,0:T(8,128)(2,1)S(1)}, bf16[2,16,64,256]{3,2,1,0:T(8,128)(2,1)}, u32[]{:S(2)}) copy-start(bf16[2,16,64,256]{3,2,1,0:T(8,128)(2,1)} %get-tuple-element.14) | copy-start | bytes 3145732

commit v2 on v1

--- a/solution.py
+++ b/solution.py
@@ -12,7 +12,6 @@
 MAMBA_COLUMNS = 8192
 MAX_PREFIX_BLOCK = 48
 PER_REQUEST = 56
-POSITIONS = 112
 TOKENS = 128
 XN, YN, CN, ZN = 4, 8, 2, 8
 UNITS = 16
@@ -43,14 +42,16 @@
 
 
 def kernel(
-    send_index, position_index, counts,
-    queries, suffix_keys, suffix_values, mamba_x, mamba_gate, b_rows, c_rows,
-    steps, decay_log, skip_lanes, norm_gain, cache,
+    counts, decay_log, skip_gain, request_units, steps_row, norm_gain,
+    queries_hbm, suffix_keys_hbm, suffix_values_hbm, mamba_x_hbm, mamba_gate_hbm, b_hbm, c_hbm,
+    cache_hbm,
     attn_out, mamba_out, final_state,
+    queries, suffix_keys, suffix_values, mamba_x, mamba_gate, b_rows, c_rows, cache,
+    table_rows, table,
     yk, yv, pick, xk, xv, kin, vin, probs, suffix_probs, scores, query_scr,
-    top, total, group_top, out_acc, products, run_col, run_row, step_row, local_y,
-    closing, square_out, square_in,
-    y_send, y_recv, x_send, x_recv, z_send, z_recv,
+    top, total, group_top, out_acc, products, run_col, step_col, run_row, step_row, local_y,
+    closing, squares, square_out, square_in,
+    y_send, y_recv, x_send, x_recv, z_send, z_recv, load_sem, table_sem,
 ):
     rep = lax.axis_index("rep")
     tp = lax.axis_index("tp")
@@ -58,6 +59,24 @@
 
     def device(dx, dy, dc):
         return (((x + dx) % XN * YN + (y + dy) % YN) * CN + (c + dc) % CN, tp)
+
+    loads = [
+        pltpu.make_async_copy(src, dst, load_sem.at[i])
+        for i, (src, dst) in enumerate(
+            (
+                (cache_hbm, cache),
+                (queries_hbm, queries),
+                (suffix_keys_hbm, suffix_keys),
+                (suffix_values_hbm, suffix_values),
+                (b_hbm, b_rows),
+                (c_hbm, c_rows),
+                (mamba_x_hbm, mamba_x),
+                (mamba_gate_hbm, mamba_gate),
+            )
+        )
+    ]
+    for load in loads:
+        load.start()
 
     barrier = pltpu.get_barrier_semaphore()
     for dx, dc in PARTNERS[1:]:
@@ -66,6 +85,44 @@
         pl.semaphore_signal(barrier, 1, device_id=device(0, dy, 0), device_id_type=MESH)
     for dz in range(1, ZN):
         pl.semaphore_signal(barrier, 1, device_id=(rep, (tp + dz) % ZN), device_id_type=MESH)
+
+    slot = lax.broadcasted_iota(jnp.int32, (PER_REQUEST, 128), 0)
+    request = lax.broadcasted_iota(jnp.int32, (PER_REQUEST, 128), 1)
+    request_row = request[:1]
+    counts_row = jnp.zeros((1, 128), jnp.int32)
+    for tx in range(XN):
+        for q in range(4):
+            at = tx * 32 + y * 4 + q
+            counts_row = jnp.where(request_row == at, counts[at], counts_row)
+    live = (slot < counts_row) | (slot >= MAX_PREFIX_BLOCK)
+    units = request_units[...]
+    owner = jnp.where(live, units >> 4, -1)
+    code = (((request & 1) * PER_REQUEST + slot) << 4) + (units & 15)
+    for dy in range(YN):
+        hit = owner == (x * YN + (y + YN - dy) % YN) * CN + c
+        table_rows[pl.ds(dy, 1)] = jnp.min(
+            jnp.where(hit, code, 1 << 20), axis=0, keepdims=True
+        )
+        table_rows[pl.ds(YN + dy, 1)] = jnp.max(jnp.where(hit, code, 0), axis=0, keepdims=True)
+    own_col, own_row = [], []
+    for q in range(2):
+        mine = jnp.where(request == rep * 2 + q, owner, 0)
+        own_col.append(jnp.sum(mine, axis=1, keepdims=True))
+        own_row.append(
+            jnp.sum(jnp.where(slot == request, own_col[q], 0), axis=0, keepdims=True)
+        )
+    for q in range(2):
+        same = (own_col[q] == own_row[q]) & (slot < request)
+        if q == 1:
+            same = same | (own_col[0] == own_row[1])
+        again = jnp.max(same.astype(jnp.int32), axis=0, keepdims=True)
+        ox, oy, oc = own_row[q] >> 4, (own_row[q] >> 1) & 7, own_row[q] & 1
+        j = ((x - ox) & 3) * CN + ((c - oc) & 1)
+        place = (j * YN + ((y - oy) & 7)) * 2 + again
+        table_rows[pl.ds(2 * YN + q, 1)] = jnp.where(own_row[q] >= 0, place, 0)
+    to_table = pltpu.make_async_copy(table_rows, table, table_sem)
+    to_table.start()
+
     pl.semaphore_wait(barrier, len(PARTNERS) - 1 + 2 + ZN - 1)
 
     ybufs, xbufs, inbufs = (yk, yv), (xk, xv), (kin, vin)
@@ -109,9 +166,10 @@
 
     def send_chosen(phase, dy):
         for j, (dx, dc) in enumerate(PARTNERS):
-            target = ((x + dx) % XN) * CN + (c + dc) % CN
-            for s in range(2):
-                unit = send_index[(dy * 8 + target) * 2 + s]
+            at = ((x + dx) % XN) * 32 + y * 4 + ((c + dc) % CN) * 2
+            first = jnp.minimum(table[dy, at], table[dy, at + 1]) & 15
+            last = jnp.maximum(table[YN + dy, at], table[YN + dy, at + 1]) & 15
+            for s, unit in enumerate((first, last)):
                 if j == 0:
                     inbufs[phase][dy * 2 + s] = pick[unit]
                 else:
@@ -119,9 +177,11 @@
             if j > 0:
                 x_copy(phase, dy, j).start()
 
-    for direction in (0, 1):
-        for ss in (0, 1):
+    loads[0].wait()
+    for ss in (0, 1):
+        for direction in (0, 1):
             y_own(0, direction, ss).start()
+    to_table.wait()
     for phase in (0, 1):
         pick[...] = cache[:, phase]
         send_chosen(phase, 0)
@@ -131,19 +191,27 @@
     low_half = lane < 64
     lane16 = lax.broadcasted_iota(jnp.int32, (TOKENS, 16), 1)
     causal = row >= lane
-    rates = -jnp.exp(decay_log[...])
+    for load in loads[1:]:
+        load.wait()
+
+    def rate(h):
+        return -jnp.exp(jnp.full((1, 128), decay_log[h], jnp.float32))
+
+    def place_of(q, position):
+        return table[2 * YN + q, position]
 
     def prepare(q, carry):
         rows = pl.ds(pl.multiple_of(q * TOKENS, TOKENS), TOKENS)
         for h in range(4):
             query_scr[q, pl.ds(h * TOKENS, TOKENS)] = queries[rows, pl.ds(h * 128, 128)]
-        delta = steps[rows, :]
+        delta = steps_row[:, rows]
         lower = (row >= lane).astype(jnp.float32)
         upper = (row <= lane).astype(jnp.float32)
         unit = (row == lane).astype(jnp.float32)
-        run_col[q] = dot_nn(lower, delta * rates, HIGHEST)
-        run_row[q] = dot_tn(delta * rates, upper, HIGHEST)
-        step_row[q] = dot_tn(delta, unit, HIGHEST)
+        run_col[q] = dot_nt(lower, delta, HIGHEST)
+        step_col[q] = dot_nt(unit, delta, HIGHEST)
+        run_row[q] = dot_nn(delta, upper, HIGHEST)
+        step_row[q] = delta
         products[q] = jnp.where(causal, dot_nt(c_rows[rows, :], b_rows[rows, :]), 0.0)
         keys = suffix_keys[rows, :]
         for h in range(4):
@@ -160,8 +228,8 @@
 
     lax.fori_loop(0, 2, prepare, 0)
 
-    def column(ref, q_rows, h):
-        return jnp.sum(jnp.where(lane16 == h, ref[q_rows], 0.0), axis=1, keepdims=True)
+    def column(table16, h):
+        return jnp.sum(jnp.where(lane16 == h, table16, 0.0), axis=1, keepdims=True)
 
     def mamba_pair(i, carry):
         q, p = i // PAIRS, i % PAIRS
@@ -170,19 +238,21 @@
         xs = mamba_x[rows, lanes]
         parts, tails = [], []
         run = run_col[q]
-        delta = steps[rows, :]
+        delta = step_col[q]
         for e in (0, 1):
             h = 2 * p + e
-            rc = jnp.sum(jnp.where(lane16 == h, run, 0.0), axis=1, keepdims=True)
-            dc = jnp.sum(jnp.where(lane16 == h, delta, 0.0), axis=1, keepdims=True)
+            rc, dc = column(run, h), column(delta, h)
             rr = run_row[q, pl.ds(h, 1)]
             dr = step_row[q, pl.ds(h, 1)]
-            gaps = jnp.where(causal, rc - rr, NEG)
+            rh = rate(h)
+            gaps = jnp.where(causal, (rc - rr) * rh, NEG)
             mix = jnp.exp(gaps) * products[q] * dr
             parts.append(dot_nn(mix.astype(jnp.bfloat16), xs))
-            tails.append(jnp.exp(rc[TOKENS - 1 : TOKENS] - rc) * dc)
+            tails.append(jnp.exp((rc[TOKENS - 1 : TOKENS] - rc) * rh) * dc)
         xf = xs.astype(jnp.float32)
-        local_y[rows, lanes] = jnp.where(low_half, parts[0], parts[1]) + skip_lanes[:, lanes] * xf
+        local_y[rows, lanes] = jnp.where(
+            low_half, parts[0] + skip_gain[2 * p] * xf, parts[1] + skip_gain[2 * p + 1] * xf
+        )
         weighted = (xf * jnp.where(low_half, tails[0], tails[1])).astype(jnp.bfloat16)
         closing[i] = dot_tn(weighted, b_rows[rows, :])
         return carry
@@ -190,37 +260,49 @@
     source_row = jnp.where(row < 64, 2 * row, 2 * (row - 64) + 1)
     deal = (lane == source_row).astype(jnp.bfloat16)
 
-    def state_head(phase):
-        def step(i, carry):
+    def state_heads(phase):
+        def one(i):
             q, p = i // PAIRS, i % PAIRS
             rows = pl.ds(pl.multiple_of(q * TOKENS, TOKENS), TOKENS)
             lanes = pl.ds(pl.multiple_of(p * 128, 128), 128)
             h = 2 * p + phase
-            unit = inbufs[phase][position_index[q * PER_REQUEST + MAX_PREFIX_BLOCK + p]]
+            unit = inbufs[phase][place_of(q, MAX_PREFIX_BLOCK + p)]
             dealt = dot_nn(deal, unit)
             state = jnp.concatenate([dealt[:64], dealt[64:]], axis=1)
-            rc = jnp.sum(jnp.where(lane16 == h, run_col[q], 0.0), axis=1, keepdims=True)
+            run = jnp.exp(column(run_col[q], h) * rate(h))
             blank = jnp.zeros((64, 256), jnp.bfloat16)
             sb = state.astype(jnp.bfloat16)
             both = [sb, blank] if phase == 0 else [blank, sb]
             carried = dot_nt(c_rows[rows, :], jnp.concatenate(both, axis=0))
-            local_y[rows, lanes] = local_y[rows, lanes] + jnp.exp(rc) * carried
-            last = jnp.exp(rc[TOKENS - 1 : TOKENS])
+            mixed = local_y[rows, lanes] + run * carried
+            last = run[TOKENS - 1 : TOKENS, :1]
             final_state[q, h] = (
                 last * state + closing[i, pl.ds(phase * 64, 64)]
             ).astype(jnp.bfloat16)
+            if phase == 0:
+                local_y[rows, lanes] = mixed
+                return None
+            gate = mamba_gate[rows, lanes].astype(jnp.float32)
+            gated = mixed * (gate / (1.0 + jnp.exp(-gate)))
+            local_y[rows, lanes] = gated
+            return gated * gated
+
+        def step(i, carry):
+            found = [one(i * 4 + n) for n in range(4)]
+            if phase == 1:
+                squares[i] = (found[0] + found[1]) + (found[2] + found[3])
             return carry
 
-        return step
+        lax.fori_loop(0, 4, step, 0)
 
     def score_group(i, carry):
         q, g = i // GROUPS, i % GROUPS
         qv = query_scr[q]
         for b in range(GROUP):
             block = g * GROUP + b
-            key = kin[position_index[q * PER_REQUEST + block]]
+            key = kin[place_of(q, block)]
             s = dot_nt(qv, key) * SCALING
-            scores[:, pl.ds(b * 128, 128)] = jnp.where(block < counts[q], s, NEG)
+            scores[:, pl.ds(b * 128, 128)] = jnp.where(block < counts[rep * 2 + q], s, NEG)
         for r in range(4):
             part = pl.ds(r * TOKENS, TOKENS)
             mx = scores[part, pl.ds(0, 128)]
@@ -281,39 +363,30 @@
                 lax.fori_loop(ss * 16 // 7, (ss + 1) * 16 // 7, mamba_pair, 0)
             else:
 
-                @pl.when(ss == 0)
+                @pl.when(ss == 2)
                 def _():
                     wait_in(0)
-                    lax.fori_loop(0, 16, state_head(0), 0)
-
-                @pl.when(ss > 0)
+                    state_heads(0)
+
+                @pl.when(ss > 2)
                 def _():
-                    lax.fori_loop(ss * 2 - 2, ss * 2, score_group, 0)
+                    lax.fori_loop(ss - 3, ss - 2, score_group, 0)
 
             return carry
 
         lax.fori_loop(0, 7, ring_step, 0)
 
+    lax.fori_loop(4, 2 * GROUPS, score_group, 0)
     for q in range(2):
         shrink = jnp.exp(group_top[q * (GROUPS + 1) + GROUPS] - top[q])
         out_acc[q] = shrink * dot_nn(suffix_probs[q], suffix_values[pl.ds(q * TOKENS, TOKENS), :])
 
     wait_in(1)
-    lax.fori_loop(0, 16, state_head(1), 0)
+    state_heads(1)
 
     ones8 = jnp.ones((8, 128), jnp.float32)
     for q in range(2):
-        rows = pl.ds(q * TOKENS, TOKENS)
-
-        def gate_pair(p, squares, rows=rows):
-            lanes = pl.ds(pl.multiple_of(p * 128, 128), 128)
-            gate = mamba_gate[rows, lanes].astype(jnp.float32)
-            gated = local_y[rows, lanes] * (gate / (1.0 + jnp.exp(-gate)))
-            local_y[rows, lanes] = gated
-            return squares + gated * gated
-
-        squares = lax.fori_loop(0, PAIRS, gate_pair, jnp.zeros((TOKENS, 128), jnp.float32))
-        square_out[q] = dot_nt(ones8, squares, HIGHEST)
+        square_out[q] = dot_nt(ones8, squares[2 * q] + squares[2 * q + 1], HIGHEST)
 
     def z_copy(dz):
         return pltpu.make_async_remote_copy(
@@ -330,7 +403,7 @@
 
     def blend_group(i, carry):
         q, g = i // GROUPS, i % GROUPS
-        values = [vin[position_index[q * PER_REQUEST + g * GROUP + b]] for b in range(GROUP)]
+        values = [vin[place_of(q, g * GROUP + b)] for b in range(GROUP)]
         blended = dot_nn(probs[i], jnp.concatenate(values, axis=0))
         out_acc[q] = out_acc[q] + jnp.exp(group_top[q * (GROUPS + 1) + g] - top[q]) * blended
         return carry
@@ -343,6 +416,7 @@
             attn_out[pl.ds(q * TOKENS, TOKENS), pl.ds(h * 128, 128)] = (
                 out_acc[q, part] / weight
             ).astype(jnp.bfloat16)
+
 
     for dz in range(1, ZN):
         z_copy(dz).wait_recv()
@@ -383,33 +457,12 @@
         z_copy(dz).wait_send()
 
 
-def tables(request_units, prefix_block_count):
-    rep = lax.axis_index("rep")
-    x, y, c = rep // 16, (rep // 2) % YN, rep % 2
-    slot = jnp.arange(PER_REQUEST, dtype=jnp.int32)
-    live = (slot[None, :] < prefix_block_count[:, None]) | (slot[None, :] >= MAX_PREFIX_BLOCK)
-    owner = jnp.where(live, request_units // UNITS, -1).reshape(XN, YN, CN, POSITIONS)
-    local = (request_units % UNITS).reshape(XN, YN, CN, POSITIONS)
-    owner = lax.dynamic_index_in_dim(owner, y, 1, keepdims=False).reshape(XN * CN, POSITIONS)
-    local = lax.dynamic_index_in_dim(local, y, 1, keepdims=False).reshape(XN * CN, POSITIONS)
-    distance = jnp.arange(YN, dtype=jnp.int32)
-    sources = (x * YN + (y - distance + YN) % YN) * CN + c
-    ordinal = jnp.arange(POSITIONS, dtype=jnp.int32)
-    code = ordinal[None, :] * UNITS + local
-    hit = owner[None] == sources[:, None, None]
-    first = jnp.min(jnp.where(hit, code[None], POSITIONS * UNITS), axis=2) % UNITS
-    last = jnp.max(jnp.where(hit, code[None], 0), axis=2) % UNITS
-    send_index = jnp.stack([first, last], axis=2).reshape(-1)
-    own = lax.dynamic_index_in_dim(owner, x * CN + c, 0, keepdims=False)
-    again = jnp.any(
-        (own[:, None] == own[None, :]) & (ordinal[None, :] < ordinal[:, None]), axis=1
-    ).astype(jnp.int32)
-    ox, oy, oc = own // 16, (own // 2) % YN, own % 2
-    j = ((x - ox + XN) % XN) * CN + (c - oc + CN) % CN
-    position_index = (j * YN + (y - oy + YN) % YN) * 2 + again
-    position_index = jnp.where(own >= 0, position_index, 0)
-    counts = lax.dynamic_slice_in_dim(prefix_block_count, rep * 2, 2)
-    return send_index, position_index, counts
+def hand_over(*refs):
+    copies = [pltpu.make_async_copy(refs[i], refs[3 + i], refs[6].at[i]) for i in range(3)]
+    for copy in copies:
+        copy.start()
+    for copy in copies:
+        copy.wait()
 
 
 def body(
@@ -417,20 +470,31 @@
     output_projection, step_lengths, decay_log, skip_gain, gated_norm_gain, cache_store,
     request_units, prefix_block_count,
 ):
-    send_index, position_index, counts = tables(request_units, prefix_block_count)
     bf16, f32 = jnp.bfloat16, jnp.float32
     vmem = pl.BlockSpec(memory_space=pltpu.VMEM)
     smem = pl.BlockSpec(memory_space=pltpu.SMEM)
-    return pl.pallas_call(
+    anywhere = pl.BlockSpec(memory_space=pl.ANY)
+    shapes = (
+        jax.ShapeDtypeStruct((256, 512), bf16),
+        jax.ShapeDtypeStruct((256, 1024), bf16),
+        jax.ShapeDtypeStruct((2, 16, 64, 256), bf16),
+    )
+    results = pl.pallas_call(
         kernel,
-        out_shape=(
-            jax.ShapeDtypeStruct((256, 512), bf16),
-            jax.ShapeDtypeStruct((256, 1024), bf16),
-            jax.ShapeDtypeStruct((2, 16, 64, 256), bf16),
-        ),
-        in_specs=[smem] * 3 + [vmem] * 12,
+        out_shape=tuple(pltpu.VMEM(s.shape, s.dtype) for s in shapes),
+        in_specs=[smem] * 3 + [vmem] * 3 + [anywhere] * 8,
         out_specs=[vmem] * 3,
         scratch_shapes=[
+            pltpu.VMEM((256, 512), bf16),
+            pltpu.VMEM((256, 128), bf16),
+            pltpu.VMEM((256, 128), bf16),
+            pltpu.VMEM((256, 1024), bf16),
+            pltpu.VMEM((256, 1024), bf16),
+            pltpu.VMEM((256, 256), bf16),
+            pltpu.VMEM((256, 256), bf16),
+            pltpu.VMEM((UNITS, 2, 128, 128), bf16),
+            pltpu.VMEM((24, 128), jnp.int32),
+            pltpu.SMEM((24, 128), jnp.int32),
             pltpu.VMEM((7, UNITS, 128, 128), bf16),
             pltpu.VMEM((7, UNITS, 128, 128), bf16),
             pltpu.VMEM((UNITS, 128, 128), bf16),
@@ -448,10 +512,12 @@
             pltpu.VMEM((2, ROWS, 128), f32),
             pltpu.VMEM((2, 128, 128), f32),
             pltpu.VMEM((2, 128, 16), f32),
+            pltpu.VMEM((2, 128, 16), f32),
             pltpu.VMEM((2, 16, 128), f32),
             pltpu.VMEM((2, 16, 128), f32),
             pltpu.VMEM((256, 1024), f32),
             pltpu.VMEM((16, 128, 256), f32),
+            pltpu.VMEM((4, 128, 128), f32),
             pltpu.VMEM((2, 8, 128), f32),
             pltpu.VMEM((7, 2, 8, 128), f32),
             pltpu.SemaphoreType.DMA((28,)),
@@ -460,16 +526,24 @@
             pltpu.SemaphoreType.DMA((112,)),
             pltpu.SemaphoreType.DMA((7,)),
             pltpu.SemaphoreType.DMA((7,)),
+            pltpu.SemaphoreType.DMA((8,)),
+            pltpu.SemaphoreType.DMA,
         ],
         compiler_params=pltpu.CompilerParams(
-            collective_id=0, has_side_effects=True, vmem_limit_bytes=62 << 20
+            collective_id=0, has_side_effects=True, vmem_limit_bytes=56 << 20
         ),
     )(
-        send_index, position_index, counts,
-        queries, suffix_key_rows, suffix_value_rows, mamba_input, mamba_gate, input_projection,
-        output_projection, step_lengths, decay_log[None], jnp.repeat(skip_gain, 64)[None],
-        gated_norm_gain[None], cache_store.reshape(UNITS, 2, 128, 128),
+        prefix_block_count, decay_log, skip_gain, request_units.T, step_lengths.T,
+        gated_norm_gain[None], queries, suffix_key_rows, suffix_value_rows, mamba_input, mamba_gate,
+        input_projection, output_projection, cache_store.reshape(UNITS, 2, 128, 128),
     )
+    return pl.pallas_call(
+        hand_over,
+        out_shape=shapes,
+        in_specs=[vmem] * 3,
+        out_specs=[anywhere] * 3,
+        scratch_shapes=[pltpu.SemaphoreType.DMA((3,))],
+    )(*(pltpu.with_memory_space_constraint(r, pltpu.VMEM) for r in results))
 
 
 def solution(mesh):

time: 146 us -> 123 us (0.84)
  Pallas kernels: 134 us -> 122 us
  local copies, waits for them, and re-layouts: 9.25 us -> 0 us
    pallas_call x1 -> x2, Pallas kernels: 134 us -> 122 us  [the longest x1 121 us: body(): pl.pallas_call(kernel, out_shape=tuple((pltpu.VMEM(s.shape, s.dtype) for...]
    unnamed x14 -> x0, local copies, waits for them, and re-layouts: 6.68 us -> none
where the time goes in v2:
time: 123 us
  Pallas kernels  122 us (99%)
    pallas_call x1, Pallas kernels, body(): pl.pallas_call(kernel, out_shape=tuple((pltpu.VMEM(s.shape, s.dtype) for...  121 us

profile of v2, /device:TPU:1, one launch (start us, length us, event | category | flops | bytes accessed | tf_op | source)
XLA Modules:
  0.0 122.6 jit_solution(10243845687112301801)
XLA Ops:
  0.6 120.7 %shard_map.157 = (bf16[256,512]{1,0:T(8,128)(2,1)S(1)}, bf16[256,1024]{1,0:T(8,128)(2,1)S(1)}, bf16[2,16,64,256]{3,2,1,0:T(8,128)(2,1)S(1)}) custom-call(s32[128]{0:T(128)} %counts.1, f32[16]{0:T(128)} %decay_log.1, f32[16]{0:T(128)} %skip_gain.1, s32[56,128]{1,0:T(8,128)} %bitcast.5, f32[16,256]{1,0:T(8,128)} %bitcast.6, f32[1,1024]{1,0:T(1,128)} %bitcast.7, ...), custom_call_target="tpu_custom_call" | custom-call | tf_op jit(solution)/shard_map/pallas_call | solution.py:482
  121.3 1.3 %shard_map.158 = (bf16[256,512]{1,0:T(8,128)(2,1)}, bf16[256,1024]{1,0:T(8,128)(2,1)}, bf16[2,16,64,256]{3,2,1,0:T(8,128)(2,1)}) custom-call(bf16[256,512]{1,0:T(8,128)(2,1)S(1)} %get-tuple-element.6.refs_0_, bf16[256,1024]{1,0:T(8,128)(2,1)S(1)} %get-tuple-element.7.refs_1_, bf16[2,16,64,256]{3,2,1,0:T(8,128)(2,1)S(1)} %get-tuple-element.8.refs_2_), custom_call_target="tpu_custom_call" | custom-call | tf_op jit(solution)/shard_map/pallas_call | solution.py:540

commit v3 on v2

--- a/solution.py
+++ b/solution.py
@@ -22,6 +22,7 @@
 NEG = -1e30
 HIGHEST = lax.Precision.HIGHEST
 SCALING = 1.0 / math.sqrt(HEAD_WIDTH)
+SEND_ORDER = (0, 4, 5, 2, 3, 6, 7, 1)
 PARTNERS = [(dx, dc) for dx in range(XN) for dc in range(CN)]
 
 
@@ -50,6 +51,7 @@
     table_rows, table,
     yk, yv, pick, xk, xv, kin, vin, probs, suffix_probs, scores, query_scr,
     top, total, group_top, out_acc, products, run_col, step_col, run_row, step_row, local_y,
+    decay_lanes, gate_lanes,
     closing, squares, square_out, square_in,
     y_send, y_recv, x_send, x_recv, z_send, z_recv, load_sem, table_sem,
 ):
@@ -59,6 +61,14 @@
 
     def device(dx, dy, dc):
         return (((x + dx) % XN * YN + (y + dy) % YN) * CN + (c + dc) % CN, tp)
+
+    barrier = pltpu.get_barrier_semaphore()
+    for dx, dc in PARTNERS[1:]:
+        pl.semaphore_signal(barrier, 1, device_id=device(dx, 0, dc), device_id_type=MESH)
+    for dy in (1, YN - 1):
+        pl.semaphore_signal(barrier, 1, device_id=device(0, dy, 0), device_id_type=MESH)
+    for dz in range(1, ZN):
+        pl.semaphore_signal(barrier, 1, device_id=(rep, (tp + dz) % ZN), device_id_type=MESH)
 
     loads = [
         pltpu.make_async_copy(src, dst, load_sem.at[i])
@@ -77,14 +87,6 @@
     ]
     for load in loads:
         load.start()
-
-    barrier = pltpu.get_barrier_semaphore()
-    for dx, dc in PARTNERS[1:]:
-        pl.semaphore_signal(barrier, 1, device_id=device(dx, 0, dc), device_id_type=MESH)
-    for dy in (1, YN - 1):
-        pl.semaphore_signal(barrier, 1, device_id=device(0, dy, 0), device_id_type=MESH)
-    for dz in range(1, ZN):
-        pl.semaphore_signal(barrier, 1, device_id=(rep, (tp + dz) % ZN), device_id_type=MESH)
 
     slot = lax.broadcasted_iota(jnp.int32, (PER_REQUEST, 128), 0)
     request = lax.broadcasted_iota(jnp.int32, (PER_REQUEST, 128), 1)
@@ -165,7 +167,8 @@
         )
 
     def send_chosen(phase, dy):
-        for j, (dx, dc) in enumerate(PARTNERS):
+        for j in SEND_ORDER:
+            dx, dc = PARTNERS[j]
             at = ((x + dx) % XN) * 32 + y * 4 + ((c + dc) % CN) * 2
             first = jnp.minimum(table[dy, at], table[dy, at + 1]) & 15
             last = jnp.maximum(table[YN + dy, at], table[YN + dy, at + 1]) & 15
@@ -236,7 +239,7 @@
         rows = pl.ds(pl.multiple_of(q * TOKENS, TOKENS), TOKENS)
         lanes = pl.ds(pl.multiple_of(p * 128, 128), 128)
         xs = mamba_x[rows, lanes]
-        parts, tails = [], []
+        parts, tails, runs = [], [], []
         run = run_col[q]
         delta = step_col[q]
         for e in (0, 1):
@@ -248,6 +251,7 @@
             gaps = jnp.where(causal, (rc - rr) * rh, NEG)
             mix = jnp.exp(gaps) * products[q] * dr
             parts.append(dot_nn(mix.astype(jnp.bfloat16), xs))
+            runs.append(rc * rh)
             tails.append(jnp.exp((rc[TOKENS - 1 : TOKENS] - rc) * rh) * dc)
         xf = xs.astype(jnp.float32)
         local_y[rows, lanes] = jnp.where(
@@ -255,6 +259,9 @@
         )
         weighted = (xf * jnp.where(low_half, tails[0], tails[1])).astype(jnp.bfloat16)
         closing[i] = dot_tn(weighted, b_rows[rows, :])
+        decay_lanes[rows, lanes] = jnp.exp(jnp.where(low_half, runs[0], runs[1]))
+        gate = mamba_gate[rows, lanes].astype(jnp.float32)
+        gate_lanes[rows, lanes] = gate / (1.0 + jnp.exp(-gate))
         return carry
 
     source_row = jnp.where(row < 64, 2 * row, 2 * (row - 64) + 1)
@@ -269,21 +276,20 @@
             unit = inbufs[phase][place_of(q, MAX_PREFIX_BLOCK + p)]
             dealt = dot_nn(deal, unit)
             state = jnp.concatenate([dealt[:64], dealt[64:]], axis=1)
-            run = jnp.exp(column(run_col[q], h) * rate(h))
+            run = decay_lanes[rows, lanes]
             blank = jnp.zeros((64, 256), jnp.bfloat16)
             sb = state.astype(jnp.bfloat16)
             both = [sb, blank] if phase == 0 else [blank, sb]
             carried = dot_nt(c_rows[rows, :], jnp.concatenate(both, axis=0))
             mixed = local_y[rows, lanes] + run * carried
-            last = run[TOKENS - 1 : TOKENS, :1]
+            last = run[TOKENS - 1 : TOKENS, phase * 64 : phase * 64 + 1]
             final_state[q, h] = (
                 last * state + closing[i, pl.ds(phase * 64, 64)]
             ).astype(jnp.bfloat16)
             if phase == 0:
                 local_y[rows, lanes] = mixed
                 return None
-            gate = mamba_gate[rows, lanes].astype(jnp.float32)
-            gated = mixed * (gate / (1.0 + jnp.exp(-gate)))
+            gated = mixed * gate_lanes[rows, lanes]
             local_y[rows, lanes] = gated
             return gated * gated
 
@@ -363,14 +369,14 @@
                 lax.fori_loop(ss * 16 // 7, (ss + 1) * 16 // 7, mamba_pair, 0)
             else:
 
-                @pl.when(ss == 2)
+                @pl.when(ss == 3)
                 def _():
                     wait_in(0)
                     state_heads(0)
 
-                @pl.when(ss > 2)
+                @pl.when((ss == 4) | (ss == 5))
                 def _():
-                    lax.fori_loop(ss - 3, ss - 2, score_group, 0)
+                    lax.fori_loop(ss * 2 - 8, ss * 2 - 6, score_group, 0)
 
             return carry
 
@@ -516,6 +522,8 @@
             pltpu.VMEM((2, 16, 128), f32),
             pltpu.VMEM((2, 16, 128), f32),
             pltpu.VMEM((256, 1024), f32),
+            pltpu.VMEM((256, 1024), f32),
+            pltpu.VMEM((256, 1024), f32),
             pltpu.VMEM((16, 128, 256), f32),
             pltpu.VMEM((4, 128, 128), f32),
             pltpu.VMEM((2, 8, 128), f32),

time: 123 us -> 122 us (level)
  no operation moved by 1% of the time
where the time goes in v3:
time: 122 us
  Pallas kernels  121 us (99%)
    pallas_call x1, Pallas kernels, body(): pl.pallas_call(kernel, out_shape=tuple((pltpu.VMEM(s.shape, s.dtype) for...  120 us

profile of v3, /device:TPU:1, one launch (start us, length us, event | category | flops | bytes accessed | tf_op | source)
XLA Modules:
  0.0 121.8 jit_solution(7708825827845834129)
XLA Ops:
  0.6 119.9 %shard_map.157 = (bf16[256,512]{1,0:T(8,128)(2,1)S(1)}, bf16[256,1024]{1,0:T(8,128)(2,1)S(1)}, bf16[2,16,64,256]{3,2,1,0:T(8,128)(2,1)S(1)}) custom-call(s32[128]{0:T(128)} %counts.1, f32[16]{0:T(128)} %decay_log.1, f32[16]{0:T(128)} %skip_gain.1, s32[56,128]{1,0:T(8,128)} %bitcast.5, f32[16,256]{1,0:T(8,128)} %bitcast.6, f32[1,1024]{1,0:T(1,128)} %bitcast.7, ...), custom_call_target="tpu_custom_call" | custom-call | tf_op jit(solution)/shard_map/pallas_call | solution.py:488
  120.5 1.3 %shard_map.158 = (bf16[256,512]{1,0:T(8,128)(2,1)}, bf16[256,1024]{1,0:T(8,128)(2,1)}, bf16[2,16,64,256]{3,2,1,0:T(8,128)(2,1)}) custom-call(bf16[256,512]{1,0:T(8,128)(2,1)S(1)} %get-tuple-element.6.refs_0_, bf16[256,1024]{1,0:T(8,128)(2,1)S(1)} %get-tuple-element.7.refs_1_, bf16[2,16,64,256]{3,2,1,0:T(8,128)(2,1)S(1)} %get-tuple-element.8.refs_2_), custom_call_target="tpu_custom_call" | custom-call | tf_op jit(solution)/shard_map/pallas_call | solution.py:548

commit v4 on v3

--- a/solution.py
+++ b/solution.py
@@ -120,7 +120,9 @@
         again = jnp.max(same.astype(jnp.int32), axis=0, keepdims=True)
         ox, oy, oc = own_row[q] >> 4, (own_row[q] >> 1) & 7, own_row[q] & 1
         j = ((x - ox) & 3) * CN + ((c - oc) & 1)
-        place = (j * YN + ((y - oy) & 7)) * 2 + again
+        dy = (y - oy) & 7
+        chunk = jnp.where(dy < 4, 2 * dy, jnp.where(dy == 4, 1, 2 * (YN - dy) + 1))
+        place = (j * YN + chunk) * 2 + again
         table_rows[pl.ds(2 * YN + q, 1)] = jnp.where(own_row[q] >= 0, place, 0)
     to_table = pltpu.make_async_copy(table_rows, table, table_sem)
     to_table.start()
@@ -154,19 +156,19 @@
         half = half if direction == 0 else 1 - half
         return y_copy(phase, direction, ybufs[phase].at[row, pl.ds(half * 8, 8)], ss + 2)
 
-    def x_copy(phase, dy, j):
+    def x_copy(phase, at, j, chunks):
         dx, dc = PARTNERS[j]
-        slot = (phase * YN + dy) * 7 + j - 1
+        slot = (phase * YN + at) * 7 + j - 1
         return pltpu.make_async_remote_copy(
-            src_ref=xbufs[phase].at[dy, j - 1],
-            dst_ref=inbufs[phase].at[pl.ds((j * YN + dy) * 2, 2)],
+            src_ref=xbufs[phase].at[j - 1, pl.ds(at * 2, 2 * chunks)],
+            dst_ref=inbufs[phase].at[pl.ds((j * YN + at) * 2, 2 * chunks)],
             send_sem=x_send.at[slot],
             recv_sem=x_recv.at[slot],
             device_id=device(dx, 0, dc),
             device_id_type=MESH,
         )
 
-    def send_chosen(phase, dy):
+    def choose(phase, dy, place):
         for j in SEND_ORDER:
             dx, dc = PARTNERS[j]
             at = ((x + dx) % XN) * 32 + y * 4 + ((c + dc) % CN) * 2
@@ -174,11 +176,13 @@
             last = jnp.maximum(table[YN + dy, at], table[YN + dy, at + 1]) & 15
             for s, unit in enumerate((first, last)):
                 if j == 0:
-                    inbufs[phase][dy * 2 + s] = pick[unit]
+                    inbufs[phase][place * 2 + s] = pick[unit]
                 else:
-                    xbufs[phase][dy, j - 1, s] = pick[unit]
-            if j > 0:
-                x_copy(phase, dy, j).start()
+                    xbufs[phase][j - 1, place * 2 + s] = pick[unit]
+
+    def send(phase, place, chunks):
+        for j in SEND_ORDER[1:]:
+            x_copy(phase, place, j, chunks).start()
 
     loads[0].wait()
     for ss in (0, 1):
@@ -187,7 +191,8 @@
     to_table.wait()
     for phase in (0, 1):
         pick[...] = cache[:, phase]
-        send_chosen(phase, 0)
+        choose(phase, 0, 0)
+        send(phase, 0, 1)
 
     lane = lax.broadcasted_iota(jnp.int32, (TOKENS, 128), 1)
     row = lax.broadcasted_iota(jnp.int32, (TOKENS, 128), 0)
@@ -327,12 +332,15 @@
         return carry
 
     def wait_in(phase):
-        def step(dy, carry):
+        def step(k, carry):
             for j in range(1, 8):
-                x_copy(phase, dy, j).wait_recv()
+                x_copy(phase, 2 * k, j, 2).wait_recv()
             return carry
 
-        lax.fori_loop(0, YN, step, 0)
+        for j in range(1, 8):
+            x_copy(phase, 0, j, 1).wait_recv()
+            x_copy(phase, 1, j, 1).wait_recv()
+        lax.fori_loop(1, 4, step, 0)
 
     for phase in (0, 1):
 
@@ -355,15 +363,19 @@
                     def _():
                         y_own(1, direction, 1).start()
 
-            @pl.when((ss % 2 == 1) | (ss == 6))
+            @pl.when(ss == 6)
+            def _():
+                pick[...] = ybufs[phase][3]
+                choose(phase, 4, 1)
+                send(phase, 1, 1)
+
+            @pl.when(ss % 2 == 1)
             def _():
                 pick[...] = ybufs[phase][k - 1]
-                send_chosen(phase, k)
-
-            @pl.when(ss % 2 == 1)
-            def _():
+                choose(phase, k, 2 * k)
                 pick[...] = ybufs[phase][YN - 1 - k]
-                send_chosen(phase, YN - k)
+                choose(phase, YN - k, 2 * k + 1)
+                send(phase, 2 * k, 2)
 
             if phase == 0:
                 lax.fori_loop(ss * 16 // 7, (ss + 1) * 16 // 7, mamba_pair, 0)
@@ -451,14 +463,18 @@
                 y_copy(phase, direction, None, ss).wait_send()
         return carry
 
-    def drain_x(dy, carry):
+    def drain_x(k, carry):
         for phase in (0, 1):
             for j in range(1, 8):
-                x_copy(phase, dy, j).wait_send()
+                x_copy(phase, 2 * k, j, 2).wait_send()
         return carry
 
     lax.fori_loop(0, 7, drain_y, 0)
-    lax.fori_loop(0, YN, drain_x, 0)
+    for phase in (0, 1):
+        for j in range(1, 8):
+            x_copy(phase, 0, j, 1).wait_send()
+            x_copy(phase, 1, j, 1).wait_send()
+    lax.fori_loop(1, 4, drain_x, 0)
     for dz in range(1, ZN):
         z_copy(dz).wait_send()
 
@@ -504,8 +520,8 @@
             pltpu.VMEM((7, UNITS, 128, 128), bf16),
             pltpu.VMEM((7, UNITS, 128, 128), bf16),
             pltpu.VMEM((UNITS, 128, 128), bf16),
-            pltpu.VMEM((8, 7, 2, 128, 128), bf16),
-            pltpu.VMEM((8, 7, 2, 128, 128), bf16),
+            pltpu.VMEM((7, 16, 128, 128), bf16),
+            pltpu.VMEM((7, 16, 128, 128), bf16),
             pltpu.VMEM((128, 128, 128), bf16),
             pltpu.VMEM((128, 128, 128), bf16),
             pltpu.VMEM((2 * GROUPS, ROWS, GROUP * 128), bf16),

time: 122 us -> 122 us (level)
  no operation moved by 1% of the time
where the time goes in v4:
time: 122 us
  Pallas kernels  121 us (99%)
    pallas_call x1, Pallas kernels, body(): pl.pallas_call(kernel, out_shape=tuple((pltpu.VMEM(s.shape, s.dtype) for...  120 us

profile of v4, /device:TPU:1, one launch (start us, length us, event | category | flops | bytes accessed | tf_op | source)
XLA Modules:
  0.0 122.0 jit_solution(9888302121403706305)
XLA Ops:
  0.6 120.1 %shard_map.157 = (bf16[256,512]{1,0:T(8,128)(2,1)S(1)}, bf16[256,1024]{1,0:T(8,128)(2,1)S(1)}, bf16[2,16,64,256]{3,2,1,0:T(8,128)(2,1)S(1)}) custom-call(s32[128]{0:T(128)} %counts.1, f32[16]{0:T(128)} %decay_log.1, f32[16]{0:T(128)} %skip_gain.1, s32[56,128]{1,0:T(8,128)} %bitcast.5, f32[16,256]{1,0:T(8,128)} %bitcast.6, f32[1,1024]{1,0:T(1,128)} %bitcast.7, ...), custom_call_target="tpu_custom_call" | custom-call | tf_op jit(solution)/shard_map/pallas_call | solution.py:504
  120.7 1.3 %shard_map.158 = (bf16[256,512]{1,0:T(8,128)(2,1)}, bf16[256,1024]{1,0:T(8,128)(2,1)}, bf16[2,16,64,256]{3,2,1,0:T(8,128)(2,1)}) custom-call(bf16[256,512]{1,0:T(8,128)(2,1)S(1)} %get-tuple-element.6.refs_0_, bf16[256,1024]{1,0:T(8,128)(2,1)S(1)} %get-tuple-element.7.refs_1_, bf16[2,16,64,256]{3,2,1,0:T(8,128)(2,1)S(1)} %get-tuple-element.8.refs_2_), custom_call_target="tpu_custom_call" | custom-call | tf_op jit(solution)/shard_map/pallas_call | solution.py:564
